TPU v7x, 32 devices: a whole 2x2x4 slice. The times are simulated.
32 devices in a mesh: groups: 2 (over y), fsdp: 4 (over z), dp: 2 (over x), pair: 2 (over core).
Axes of the slice: x: 2, y: 2, z: 4, core: 2. Of those that a mesh axis runs over, the one named last changes fastest.
Arguments:
- hidden_input: bfloat16 [4096, 8192], P(('groups', 'fsdp', 'dp', 'pair')), parts along dimension 0, may hold values from -6 to 6
- norm_gain_vector: float32 [8192], replicated, may hold values from 0.5 to 18, as said below
- value_matrix: bfloat16 [8192, 768], P('fsdp'), may hold values from -0.0625 to 0.0625
- adapter_down_map: bfloat16 [16384, 64], P(('groups', 'fsdp')), parts along dimension 0, may hold values from -0.0625 to 0.0625
- adapter_up_map: bfloat16 [128, 768], P('groups'), parts along dimension 0, may hold values from -5 to 5
- values_gradient: bfloat16 [4096, 768], P(('groups', 'fsdp', 'dp', 'pair')), parts along dimension 0, may hold values from -6 to 6
Outputs:
- grad_hidden: bfloat16 [4096, 8192], P(('groups', 'fsdp', 'dp', 'pair')), parts along dimension 0
- grad_down: float32 [16384, 64], P(('groups', 'fsdp')), parts along dimension 0
- grad_up: float32 [128, 768], P('groups'), parts along dimension 0
There are 2 independent parts, one for each index of `groups`. A program takes and returns all parts, laid end to end along the dimension named above; an argument that names none is the same for every part. Nothing has to cross between parts.
Inputs may be any that keep to these rules, and one draw needn't show every extreme that they name: `norm_gain_vector`: positive gains.
All inputs are finite; a program needn't handle non-finite values.
Results may differ from a plain program's by a relative error of at most 0.0085.
Values may be sent and summed in bfloat16 or wider, within the bound.
A program may use at most 64 MiB of HBM per device.

v0:
```python
import math
import jax
import jax.numpy as jnp
from jax import lax
from jax.sharding import PartitionSpec as P

MODEL_WIDTH = 8192
ADAPTER_RANK = 64
norm_eps = 1e-05
adapter_scale = 2.0


def contract_last(left, right):
    return lax.dot_general(
        left, right, (((1,), (1,)), ((), ())), preferred_element_type=jnp.float32
    )


def contract_leading(left, right):
    return lax.dot_general(
        left, right, (((0,), (0,)), ((), ())), preferred_element_type=jnp.float32
    )


def local(
    hidden_input, norm_gain_vector, value_matrix, adapter_down_map, adapter_up_map, values_gradient
):
    width = hidden_input.shape[1]
    stream = hidden_input.astype(jnp.float32)
    inv_rms = lax.rsqrt(jnp.mean(stream * stream, axis=1, keepdims=True) + norm_eps)
    normalized_input = (stream * inv_rms * norm_gain_vector).astype(jnp.bfloat16)
    upward_product = (
        adapter_scale
        * jnp.dot(values_gradient, adapter_up_map.T, preferred_element_type=jnp.float32)
    ).astype(jnp.bfloat16)
    every_values, every_upward = (
        lax.all_gather(values_gradient, "fsdp", axis=0, tiled=True),
        lax.all_gather(upward_product, "fsdp", axis=0, tiled=True),
    )
    columns = contract_last(every_values, value_matrix) + contract_last(
        every_upward, adapter_down_map
    )
    gradient_normalized = lax.all_to_all(
        columns.astype(jnp.bfloat16), "fsdp", split_axis=0, concat_axis=1, tiled=True
    )
    window = normalized_input
    latent_f = jnp.dot(
        window,
        lax.all_gather(adapter_down_map, "fsdp", axis=0, tiled=True),
        preferred_element_type=jnp.float32,
    )
    scaled = gradient_normalized.astype(jnp.float32) * norm_gain_vector
    grad_stream = inv_rms * scaled - stream * (inv_rms**3 / width) * jnp.sum(
        scaled * stream, axis=1, keepdims=True
    )
    latent_code = latent_f.astype(jnp.bfloat16)
    window = normalized_input
    down_shard = lax.psum_scatter(
        contract_leading(window, upward_product), "fsdp", scatter_dimension=0, tiled=True
    )
    up_portion = adapter_scale * contract_leading(latent_code, values_gradient)
    down_shard = lax.psum(down_shard, ("dp", "pair"))
    up_full = lax.psum(up_portion, ("fsdp", "dp", "pair"))
    total = lax.psum(jnp.sum(down_shard * down_shard), "fsdp") + jnp.sum(up_full * up_full)
    factor = jnp.minimum(1.0, 0.5 * math.sqrt(MODEL_WIDTH * ADAPTER_RANK) / jnp.sqrt(total))
    return (grad_stream.astype(jnp.bfloat16), factor * down_shard, factor * up_full)


def solution(mesh):
    return jax.shard_map(
        local,
        mesh=mesh,
        in_specs=(
            P(("groups", "fsdp", "dp", "pair"), None),
            P(),
            P("fsdp", None),
            P(("groups", "fsdp"), None),
            P("groups", None),
            P(("groups", "fsdp", "dp", "pair"), None),
        ),
        out_specs=(
            P(("groups", "fsdp", "dp", "pair"), None),
            P(("groups", "fsdp"), None),
            P("groups", None),
        ),
        check_vma=False,
    )
```

profile of v0, /device:TPU:0, one launch (start us, length us, event | category | flops | bytes accessed | tf_op | source)
XLA Modules:
  0.0 322.7 jit_solution(588120099054937987)
XLA Ops:
  7.2 0.0 copy-start
  7.2 0.0 reduce-scatter.2.cloned.1.call-start
  7.2 21.6 %all_gather.9 = bf16[512,768]{1,0:T(8,128)(2,1)S(1)} all-gather(bf16[128,768]{1,0:T(8,128)(2,1)} %param.11), channel_id=1, replica_groups=mesh['groups'=2,'fsdp'=4,'dp'=2,'pair'=2] {'fsdp'}, dimensions={0}, use_global_device_ids=true | all-gather | bytes 983040 | tf_op jit(solution)/shard_map/all_gather | solution.py:37
  28.9 1.2 fusion.7
  30.1 12.0 %all_gather.10 = bf16[512,64]{0,1:T(8,128)(2,1)S(1)} all-gather(bf16[128,64]{0,1:T(8,128)(2,1)S(1)} %fusion.7), channel_id=1, replica_groups=mesh['groups'=2,'fsdp'=4,'dp'=2,'pair'=2] {'fsdp'}, dimensions={0}, use_global_device_ids=true | all-gather | bytes 81920 | tf_op jit(solution)/shard_map/all_gather | solution.py:38
  42.1 1.8 fusion.13
  43.9 0.7 add_convert_fusion
  44.6 46.4 %all_to_all.13 = bf16[4,128,2048]{2,1,0:T(8,128)(2,1)S(1)} all-to-all(bf16[4,128,2048]{2,1,0:T(8,128)(2,1)S(1)} %bitcast.16), channel_id=1, replica_groups=mesh['groups'=2,'fsdp'=4,'dp'=2,'pair'=2] {'fsdp'}, dimensions={0} | all-to-all | bytes 4194304 | tf_op jit(solution)/shard_map/all_to_all | solution.py:43
  91.1 0.5 convert_bitcast_fusion
  91.6 0.0 copy-start.2
  91.6 0.5 copy.10
  92.1 1.9 copy-done.1
  94.0 1.2 fusion
  95.2 2.2 fusion.10
  97.4 0.0 reduce-scatter.2.cloned.1.call-update
  97.4 0.0 all-gather.2.cloned.1.call-start
  97.5 0.7 all-gather.2.cloned.1.call-update
  98.2 0.0 all-reduce.3.cloned.1.call-start
  98.2 42.3 %reduce-scatter.2.cloned.1.call-done = f32[2048,64]{0,1:T(8,128)} async-done(((f32[8192,64]{0,1:T(8,128)}), f32[2048,64]{0,1:T(8,128)}) %reduce-scatter.2.cloned.1.call-update) | async-done | bytes 524304 | tf_op jit(solution)/shard_map/reduce_scatter | solution.py:58
  140.5 0.0 all-reduce.3.cloned.1.call-update
  140.6 0.0 all-reduce.5.cloned.1.call-start
  140.6 28.9 %all-gather.2.cloned.1.call-done = bf16[8192,64]{0,1:T(8,128)(2,1)} async-done(((bf16[2048,64]{0,1:T(8,128)(2,1)}), bf16[8192,64]{0,1:T(8,128)(2,1)}) %all-gather.2.cloned.1.call-update) | async-done | bytes 1048592 | tf_op jit(solution)/shard_map/all_gather | solution.py:49
  169.5 3.5 %convolution_multiply_fusion = f32[64,768]{1,0:T(8,128)} fusion(bf16[128,768]{1,0:T(8,128)(2,1)S(1)} %copy-done.4, bf16[8192,64]{0,1:T(8,128)(2,1)} %all-gather.2.cloned.1.call-done, bf16[128,8192]{1,0:T(8,128)(2,1)} %param.6, f32[8192]{0:T(1024)S(1)} %copy-done.5, f32[128]{0:T(128)S(1)} %get-tuple-element.5), kind=kOutput, calls=%fused_computation.13 | convolution fusion | flops 151052288 | bytes 3572224 | tf_op jit(solution)/shard_map/dot_general | solution.py:20
  173.0 0.0 all-reduce.5.cloned.1.call-update
  173.1 5.3 %fusion.3 = bf16[128,8192]{1,0:T(8,128)(2,1)} fusion(bf16[128,8192]{1,0:T(8,128)(2,1)} %param.6, f32[128,8192]{1,0:T(8,128)} %bitcast.15, f32[128]{0:T(128)S(1)} %get-tuple-element.4, f32[128]{0:T(128)S(1)} %get-tuple-element.6, f32[8192]{0:T(1024)S(1)} %copy-done.5, f32[128]{0:T(128)S(1)} %get-tuple-element.5), kind=kLoop, calls=%fused_computation.7 | loop fusion | flops 7340032 | bytes 8422912 | tf_op jit(solution)/shard_map/convert_element_type | solution.py:66
  178.4 26.3 %all-reduce.3.cloned.1.call-done = f32[2048,64]{0,1:T(8,128)} async-done(((f32[2048,64]{0,1:T(8,128)}), f32[2048,64]{0,1:T(8,128)}) %all-reduce.3.cloned.1.call-update) | async-done | bytes 524304 | tf_op jit(solution)/shard_map/psum | solution.py:62
  204.7 1.8 multiply_reduce_fusion
  206.5 92.0 %all-reduce.5.cloned.1.call-done = f32[64,768]{1,0:T(8,128)} async-done(((f32[64,768]{1,0:T(8,128)}), f32[64,768]{1,0:T(8,128)}) %all-reduce.5.cloned.1.call-update) | async-done | bytes 196624 | tf_op jit(solution)/shard_map/psum | solution.py:63
  298.5 1.6 multiply_reduce_fusion.1
  300.1 11.2 %psum.22 = f32[]{:T(128)} all-reduce(f32[]{:T(128)} %multiply_reduce_fusion), channel_id=1, replica_groups=mesh['groups'=2,'fsdp'=4,'dp'=2,'pair'=2] {'fsdp'}, use_global_device_ids=true, to_apply=%region_5.0 | all-reduce | flops 1 | bytes 8 | tf_op jit(solution)/shard_map/psum | solution.py:64
  312.7 1.9 broadcast_multiply_fusion
  314.6 1.6 broadcast_multiply_fusion.1
  (10 shorter events, 0.0 us)
Async XLA Ops:
  7.2 34.9 %copy-start = (bf16[2048,768]{1,0:T(8,128)(2,1)S(1)}, bf16[2048,768]{1,0:T(8,128)(2,1)}, u32[]{:S(2)}) copy-start(bf16[2048,768]{1,0:T(8,128)(2,1)} %param.8) | copy-start | bytes 9437188
  7.2 133.4 %reduce-scatter.2.cloned.1.call-start = ((), (), s32[]{:S(2)}) async-start(), calls=%async_computation.2 | async-start | bytes 2621440 | tf_op jit(solution)/shard_map/reduce_scatter | solution.py:58
  42.1 1.8 copy-start.3
  91.6 2.5 copy-start.2
  91.6 2.4 copy-start.5
  92.1 1.9 copy-start.1
  95.2 74.3 %copy-start.4 = (bf16[128,768]{1,0:T(8,128)(2,1)S(1)}, bf16[128,768]{1,0:T(8,128)(2,1)}, u32[]{:S(2)}) copy-start(bf16[128,768]{1,0:T(8,128)(2,1)} %param.11) | copy-start | bytes 589828
  97.4 72.1 %all-gather.2.cloned.1.call-start = ((), (), s32[]{:S(2)}) async-start(), calls=%async_computation.4 | async-start | bytes 1310720 | tf_op jit(solution)/shard_map/all_gather | solution.py:49
  98.2 106.5 %all-reduce.3.cloned.1.call-start = ((), (), s32[]{:S(2)}) async-start(), calls=%async_computation.3 | async-start | bytes 1048576 | tf_op jit(solution)/shard_map/psum | solution.py:62
  140.6 157.9 %all-reduce.5.cloned.1.call-start = ((), (), s32[]{:S(2)}) async-start(), calls=%async_computation.5 | async-start | bytes 393216 | tf_op jit(solution)/shard_map/psum | solution.py:63
Sparse Core Ops, SparseCore 0:
  97.6 42.9 reduce-scatter.1
  142.2 27.2 all-gather.1
  172.0 32.6 all-reduce.2
  208.9 89.5 all-reduce.4
where the time goes:
time: 323 us
  waiting for transfers between devices  190 us (59%)
  blocking collectives  91.3 us (28%)
  between operations  15.2 us (5%)
  other arithmetic  13.9 us (4%)
  matrix products  9.43 us (3%)
    psum x1, waiting for transfers between devices, local(): up_full = lax.psum(up_portion, ('fsdp', 'dp', 'pair'))  92 us
    all_to_all x1, blocking collectives, local(): lax.all_to_all(columns.astype(jnp.bfloat16), 'fsdp', split_axis=0, concat...  46.4 us
    reduce_scatter x1, waiting for transfers between devices, local(): lax.psum_scatter(contract_leading(window, upward_product), 'fsdp', scatte...  42.3 us
    all_gather x1, waiting for transfers between devices, local(): lax.all_gather(adapter_down_map, 'fsdp', axis=0, tiled=True)  28.9 us
    psum x1, waiting for transfers between devices, local(): down_shard = lax.psum(down_shard, ('dp', 'pair'))  26.3 us
    all_gather x1, blocking collectives, local(): lax.all_gather(values_gradient, 'fsdp', axis=0, tiled=True)  21.6 us
    all_gather x1, blocking collectives, local(): lax.all_gather(upward_product, 'fsdp', axis=0, tiled=True)  12 us
    psum x1, blocking collectives, local(): lax.psum(jnp.sum(down_shard * down_shard), 'fsdp')  11.2 us
  transfers between devices with their start and end apart: 4, of which 4 were waited for; matrix products, arithmetic and copies ran while one was open for 3% of the time, Pallas kernels for 0%

commit v1 on v0

--- a/solution.py
+++ b/solution.py
@@ -8,6 +8,22 @@
 ADAPTER_RANK = 64
 norm_eps = 1e-05
 adapter_scale = 2.0
+
+
+def gather_around(x, axis, dim):
+    ways, here, hop = (lax.axis_size(axis), lax.axis_index(axis), x.shape[dim])
+    lengths = [n * ways if d == dim else n for d, n in enumerate(x.shape)]
+    full = lax.dynamic_update_slice_in_dim(jnp.zeros(lengths, x.dtype), x, here * hop, axis=dim)
+    going_up = going_down = x
+    for far in range(1, ways // 2 + 1):
+        going_up = lax.ppermute(going_up, axis, [(d, (d + 1) % ways) for d in range(ways)])
+        full = lax.dynamic_update_slice_in_dim(full, going_up, (here - far) % ways * hop, axis=dim)
+        if 2 * far < ways:
+            going_down = lax.ppermute(going_down, axis, [(d, (d - 1) % ways) for d in range(ways)])
+            full = lax.dynamic_update_slice_in_dim(
+                full, going_down, (here + far) % ways * hop, axis=dim
+            )
+    return full
 
 
 def contract_last(left, right):
@@ -34,7 +50,7 @@
         * jnp.dot(values_gradient, adapter_up_map.T, preferred_element_type=jnp.float32)
     ).astype(jnp.bfloat16)
     every_values, every_upward = (
-        lax.all_gather(values_gradient, "fsdp", axis=0, tiled=True),
+        gather_around(values_gradient, "fsdp", 0),
         lax.all_gather(upward_product, "fsdp", axis=0, tiled=True),
     )
     columns = contract_last(every_values, value_matrix) + contract_last(

time: 323 us -> 323 us (level)
  blocking collectives: 91.3 us -> 73.2 us
  starting transfers between devices: 0.16 us -> 6.51 us
  waiting for transfers between devices: 190 us -> 196 us
  matrix products: 9.43 us -> 14.5 us
    all_gather x1 -> x0, blocking collectives: 21.6 us -> none  [local(): lax.all_gather(values_gradient, 'fsdp', axis=0, tiled=True)]
    ppermute x0 -> x3, starting transfers between devices: none -> 6.36 us  [the longest x2 4.27 us: gather_around(): lax.ppermute(going_up, axis, [(d, (d + 1) % ways) for d in range(ways)])]
    ppermute x0 -> x3, waiting for transfers between devices: none -> 5.35 us  [the longest x2 5.35 us: gather_around(): lax.ppermute(going_up, axis, [(d, (d + 1) % ways) for d in range(ways)])]
    dot_general x2, matrix products: 2.55 us -> 7.65 us  [contract_last(): lax.dot_general(left, right, (((1,), (1,)), ((), ())), preferred_element_...]
  transfers between devices with their start and end apart: 4 -> 7, of which waited for: 4 -> 5; matrix products, arithmetic and copies ran while one was open for 3% -> 5% of each run, Pallas kernels for 0% -> 0%
where the time goes in v1:
time: 323 us; the launch traced here: 322 us
  waiting for transfers between devices  196 us (61%)
  blocking collectives  73.2 us (23%)
  between operations  15.2 us (5%)
  matrix products  14.5 us (4%)
  other arithmetic  13.9 us (4%)
  starting transfers between devices  6.51 us (2%)
  local copies, waits for them, and re-layouts  3.49 us (1%)
    psum x1, waiting for transfers between devices, local(): up_full = lax.psum(up_portion, ('fsdp', 'dp', 'pair'))  92 us
    all_to_all x1, blocking collectives, local(): lax.all_to_all(columns.astype(jnp.bfloat16), 'fsdp', split_axis=0, concat...  47.7 us
    reduce_scatter x1, waiting for transfers between devices, local(): lax.psum_scatter(contract_leading(window, upward_product), 'fsdp', scatte...  42.3 us
    all_gather x1, waiting for transfers between devices, local(): lax.all_gather(adapter_down_map, 'fsdp', axis=0, tiled=True)  28.9 us
    psum x1, waiting for transfers between devices, local(): down_shard = lax.psum(down_shard, ('dp', 'pair'))  26.3 us
    all_gather x1, blocking collectives, local(): lax.all_gather(upward_product, 'fsdp', axis=0, tiled=True)  14.3 us
    psum x1, blocking collectives, local(): lax.psum(jnp.sum(down_shard * down_shard), 'fsdp')  11.2 us
    dot_general x2, matrix products, contract_last(): lax.dot_general(left, right, (((1,), (1,)), ((), ())), preferred_element_...  7.65 us
  transfers between devices with their start and end apart: 7, of which 5 were waited for; matrix products, arithmetic and copies ran while one was open for 5% of the time, Pallas kernels for 0%

profile of v1, /device:TPU:0, one launch (start us, length us, event | category | flops | bytes accessed | tf_op | source)
XLA Modules:
  0.0 322.5 jit_solution(8233561451906112992)
XLA Ops:
  7.2 0.0 reduce-scatter.2.cloned.1.call-start
  7.2 3.1 collective-permute-start
  10.3 2.1 collective-permute-start.1
  12.4 1.2 fusion.7
  13.6 14.3 %all_gather.6 = bf16[512,64]{0,1:T(8,128)(2,1)S(1)} all-gather(bf16[128,64]{0,1:T(8,128)(2,1)S(1)} %fusion.7), channel_id=1, replica_groups=mesh['groups'=2,'fsdp'=4,'dp'=2,'pair'=2] {'fsdp'}, dimensions={0}, use_global_device_ids=true | all-gather | bytes 81920 | tf_op jit(solution)/shard_map/all_gather | solution.py:54
  27.9 3.6 %fusion.13 = f32[512,2048]{1,0:T(8,128)} fusion(bf16[512,64]{0,1:T(8,128)(2,1)S(1)} %all_gather.6, bf16[2048,64]{0,1:T(8,128)(2,1)} %param.9), kind=kOutput, calls=%fused_computation.29 | convolution fusion | flops 134217728 | bytes 4521984 | tf_op jit(solution)/shard_map/dot_general | solution.py:30
  31.5 0.1 broadcast_in_dim.2
  31.6 1.2 collective-permute-start.2
  32.8 0.9 constant_dynamic-update-slice_fusion.1
  33.7 5.3 %collective-permute-done.2 = bf16[128,768]{1,0:T(8,128)(2,1)S(1)} collective-permute-done((bf16[128,768]{1,0:T(8,128)(2,1)S(1)}, bf16[128,768]{1,0:T(8,128)(2,1)S(1)}, u32[]{:S(2)}, u32[]{:S(2)}) %collective-permute-start.2) | collective-permute-done | bytes 196640 | tf_op jit(solution)/shard_map/ppermute | solution.py:19
  39.1 4.1 %add_convert_fusion = bf16[512,2048]{1,0:T(8,128)(2,1)S(1)} fusion(f32[512,2048]{1,0:T(8,128)} %fusion.13, bf16[512,768]{1,0:T(8,128)(2,1)S(1)} %constant_dynamic-update-slice_fusion, bf16[2048,768]{1,0:T(8,128)(2,1)S(1)} %copy-done), kind=kOutput, calls=%fused_computation.12 | convolution fusion | flops 1612709888 | bytes 10223616 | tf_op jit(solution)/shard_map/dot_general | solution.py:30
  43.2 47.7 %all_to_all.13 = bf16[4,128,2048]{2,1,0:T(8,128)(2,1)S(1)} all-to-all(bf16[4,128,2048]{2,1,0:T(8,128)(2,1)S(1)} %bitcast.16), channel_id=1, replica_groups=mesh['groups'=2,'fsdp'=4,'dp'=2,'pair'=2] {'fsdp'}, dimensions={0} | all-to-all | bytes 4194304 | tf_op jit(solution)/shard_map/all_to_all | solution.py:59
  90.9 0.5 convert_bitcast_fusion
  91.5 0.5 copy.10
  92.0 1.9 copy-done.1
  93.9 1.2 fusion
  95.1 2.2 fusion.10
  97.3 0.0 all-gather.2.cloned.1.call-start
  97.3 0.7 all-gather.2.cloned.1.call-update
  98.0 0.0 all-reduce.3.cloned.1.call-start
  98.1 42.3 %reduce-scatter.2.cloned.1.call-done = f32[2048,64]{0,1:T(8,128)} async-done(((f32[8192,64]{0,1:T(8,128)}), f32[2048,64]{0,1:T(8,128)}) %reduce-scatter.2.cloned.1.call-update) | async-done | bytes 524304 | tf_op jit(solution)/shard_map/reduce_scatter | solution.py:74
  140.3 0.0 all-reduce.5.cloned.1.call-start
  140.4 28.9 %all-gather.2.cloned.1.call-done = bf16[8192,64]{0,1:T(8,128)(2,1)} async-done(((bf16[2048,64]{0,1:T(8,128)(2,1)}), bf16[8192,64]{0,1:T(8,128)(2,1)}) %all-gather.2.cloned.1.call-update) | async-done | bytes 1048592 | tf_op jit(solution)/shard_map/all_gather | solution.py:65
  169.3 3.5 %convolution_multiply_fusion = f32[64,768]{1,0:T(8,128)} fusion(bf16[128,768]{1,0:T(8,128)(2,1)S(1)} %copy-done.3, bf16[8192,64]{0,1:T(8,128)(2,1)} %all-gather.2.cloned.1.call-done, bf16[128,8192]{1,0:T(8,128)(2,1)} %param.6, f32[8192]{0:T(1024)S(1)} %copy-done.4, f32[128]{0:T(128)S(1)} %get-tuple-element.5), kind=kOutput, calls=%fused_computation.13 | convolution fusion | flops 151052288 | bytes 3572224 | tf_op jit(solution)/shard_map/dot_general | solution.py:36
  172.8 5.3 %fusion.3 = bf16[128,8192]{1,0:T(8,128)(2,1)} fusion(bf16[128,8192]{1,0:T(8,128)(2,1)} %param.6, f32[128,8192]{1,0:T(8,128)} %bitcast.15, f32[128]{0:T(128)S(1)} %get-tuple-element.4, f32[128]{0:T(128)S(1)} %get-tuple-element.6, f32[8192]{0:T(1024)S(1)} %copy-done.4, f32[128]{0:T(128)S(1)} %get-tuple-element.5), kind=kLoop, calls=%fused_computation.7 | loop fusion | flops 7340032 | bytes 8422912 | tf_op jit(solution)/shard_map/convert_element_type | solution.py:82
  178.2 26.3 %all-reduce.3.cloned.1.call-done = f32[2048,64]{0,1:T(8,128)} async-done(((f32[2048,64]{0,1:T(8,128)}), f32[2048,64]{0,1:T(8,128)}) %all-reduce.3.cloned.1.call-update) | async-done | bytes 524304 | tf_op jit(solution)/shard_map/psum | solution.py:78
  204.4 1.8 multiply_reduce_fusion
  206.2 92.0 %all-reduce.5.cloned.1.call-done = f32[64,768]{1,0:T(8,128)} async-done(((f32[64,768]{1,0:T(8,128)}), f32[64,768]{1,0:T(8,128)}) %all-reduce.5.cloned.1.call-update) | async-done | bytes 196624 | tf_op jit(solution)/shard_map/psum | solution.py:79
  298.3 1.6 multiply_reduce_fusion.1
  299.9 11.2 %psum.22 = f32[]{:T(128)} all-reduce(f32[]{:T(128)} %multiply_reduce_fusion), channel_id=1, replica_groups=mesh['groups'=2,'fsdp'=4,'dp'=2,'pair'=2] {'fsdp'}, use_global_device_ids=true, to_apply=%region_5.6 | all-reduce | flops 1 | bytes 8 | tf_op jit(solution)/shard_map/psum | solution.py:80
  312.4 1.6 broadcast_multiply_fusion.1
  314.0 1.9 broadcast_multiply_fusion
  (18 shorter events, 0.2 us)
Async XLA Ops:
  7.2 32.0 %copy-start = (bf16[2048,768]{1,0:T(8,128)(2,1)S(1)}, bf16[2048,768]{1,0:T(8,128)(2,1)}, u32[]{:S(2)}) copy-start(bf16[2048,768]{1,0:T(8,128)(2,1)} %param.8) | copy-start | bytes 9437188
  7.2 24.3 %copy-start.3 = (bf16[128,768]{1,0:T(8,128)(2,1)S(1)}, bf16[128,768]{1,0:T(8,128)(2,1)}, u32[]{:S(2)}) copy-start(bf16[128,768]{1,0:T(8,128)(2,1)} %param.11) | copy-start | bytes 589828
  7.2 133.1 %reduce-scatter.2.cloned.1.call-start = ((), (), s32[]{:S(2)}) async-start(), calls=%async_computation.2 | async-start | bytes 2621440 | tf_op jit(solution)/shard_map/reduce_scatter | solution.py:74
  7.2 24.3 %collective-permute-start = (bf16[128,768]{1,0:T(8,128)(2,1)}, bf16[128,768]{1,0:T(8,128)(2,1)S(1)}, u32[]{:S(2)}, u32[]{:S(2)}) collective-permute-start(bf16[128,768]{1,0:T(8,128)(2,1)} %param.11), channel_id=1, source_target_pairs={{0,4},{4,8},{8,12},{12,0},{1,5},{5,9},{9,13},{13,1},{2,6},{6,10},{... | collective-permute-start | bytes 589832 | tf_op jit(solution)/shard_map/ppermute | solution.py:19
  10.3 22.5 %collective-permute-start.1 = (bf16[128,768]{1,0:T(8,128)(2,1)}, bf16[128,768]{1,0:T(8,128)(2,1)}, u32[]{:S(2)}, u32[]{:S(2)}) collective-permute-start(bf16[128,768]{1,0:T(8,128)(2,1)} %param.11), channel_id=1, source_target_pairs={{0,12},{4,0},{8,4},{12,8},{1,13},{5,1},{9,5},{13,9},{2,14},{6,2},{... | collective-permute-start | bytes 589832 | tf_op jit(solution)/shard_map/ppermute | solution.py:22
  31.6 7.5 %collective-permute-start.2 = (bf16[128,768]{1,0:T(8,128)(2,1)S(1)}, bf16[128,768]{1,0:T(8,128)(2,1)S(1)}, u32[]{:S(2)}, u32[]{:S(2)}) collective-permute-start(bf16[128,768]{1,0:T(8,128)(2,1)S(1)} %collective-permute-done), channel_id=1, source_target_pairs={{0,4},{4,8},{8,12},{12,0},{1,5},{5,9},{9,13},{13,1},{2,6},{6,10},{... | collective-permute-start | bytes 589832 | tf_op jit(solution)/shard_map/ppermute | solution.py:19
  91.4 2.5 copy-start.2
  91.4 2.4 copy-start.4
  91.9 1.9 copy-start.1
  97.3 72.0 %all-gather.2.cloned.1.call-start = ((), (), s32[]{:S(2)}) async-start(), calls=%async_computation.4 | async-start | bytes 1310720 | tf_op jit(solution)/shard_map/all_gather | solution.py:65
  98.0 106.4 %all-reduce.3.cloned.1.call-start = ((), (), s32[]{:S(2)}) async-start(), calls=%async_computation.3 | async-start | bytes 1048576 | tf_op jit(solution)/shard_map/psum | solution.py:78
  140.3 157.9 %all-reduce.5.cloned.1.call-start = ((), (), s32[]{:S(2)}) async-start(), calls=%async_computation.5 | async-start | bytes 393216 | tf_op jit(solution)/shard_map/psum | solution.py:79
Sparse Core Ops, SparseCore 0:
  97.4 42.8 reduce-scatter.1
  142.0 27.2 all-gather.1
  171.7 32.6 all-reduce.2
  208.7 89.5 all-reduce.4
